TPU v7x, 128 devices: a whole 4x4x4 slice. The times are simulated.
128 devices in a mesh: pb: 8 (over y, core), pa: 16 (over z, x).
Axes of the slice: x: 4, y: 4, z: 4, core: 2. Of those that a mesh axis runs over, the one named last changes fastest.
Arguments:
- queries: bfloat16 [65536, 4096], P(('pb', 'pa')), may hold values from -32 to 32
- passages: bfloat16 [65536, 4096], P(('pb', 'pa')), may hold values from -32 to 32
- cluster_sizes: int32 [64], replicated, may hold values from 1 to 3, 128 in all
- positives: int32 [128, 512], P(('pb', 'pa')), may hold values from 0 to 511, each once within a row
Outputs:
- grad_queries: bfloat16 [65536, 4096], P(('pb', 'pa'))
- grad_passages: bfloat16 [65536, 4096], P(('pb', 'pa'))
- row_losses: float32 [128, 512], P(('pb', 'pa'))
Inputs may be any that keep to these rules, and one draw needn't show every extreme that they name: `cluster_sizes`: the sizes add up to 128. `positives`: each block's list names every row of 0 to 511 once.
All inputs are finite; a program needn't handle non-finite values.
Results may differ from a plain program's by a relative error of at most 0.0051.
Values may be sent and summed in bfloat16 or wider, within the bound.
A program may use at most 256 MiB of HBM per device.

v0:
```python
import jax
import jax.numpy as jnp
from jax import lax
from jax.sharding import PartitionSpec as P

KMAX = 3


LOWEST = -1e30


def from_behind(x, axis, by):
    size = lax.axis_size(axis)
    pairs = [(i, i + by) for i in range(size) if 0 <= i + by < size]
    return lax.ppermute(x, axis, pairs)


def cluster_index(cluster_sizes, block_count):
    cluster_ends = jnp.cumsum(cluster_sizes)
    blocks_all = jnp.arange(block_count, dtype=jnp.int32)
    return jnp.sum((cluster_ends[None, :] <= blocks_all[:, None]).astype(jnp.int32), axis=1)


def lookup(cluster_of, position):
    blocks_all = jnp.arange(cluster_of.shape[0], dtype=jnp.int32)
    return jnp.sum(jnp.where(blocks_all == position, cluster_of, 0))


def linked(cluster_of, first, second):
    in_range = jnp.logical_and(second >= 0, second < cluster_of.shape[0])
    return jnp.logical_and(in_range, lookup(cluster_of, second) == lookup(cluster_of, first))


def score_pair(query_block, passage_block):
    scale = float(query_block.shape[1]) ** (-0.5)
    product = lax.dot_general(
        query_block, passage_block, (((1,), (1,)), ((), ())), preferred_element_type=jnp.float32
    )
    return product * scale


def masked_scores(linked_now, query_block, passage_block):
    zero_scores = jnp.zeros((query_block.shape[0], passage_block.shape[0]), jnp.float32)
    return lax.cond(linked_now, lambda: score_pair(query_block, passage_block), lambda: zero_scores)


def masked_product(linked_now, weights, operand):
    zero_rows = jnp.zeros((weights.shape[0], operand.shape[1]), jnp.float32)
    return lax.cond(
        linked_now,
        lambda: jnp.dot(weights, operand, preferred_element_type=jnp.float32),
        lambda: zero_rows,
    )


def masked_transposed(linked_now, weights, operand):
    zero_rows = jnp.zeros((weights.shape[1], operand.shape[1]), jnp.bfloat16)
    return lax.cond(
        linked_now,
        lambda: lax.dot_general(
            weights, operand, (((0,), (0,)), ((), ())), preferred_element_type=jnp.float32
        ).astype(jnp.bfloat16),
        lambda: zero_rows,
    )


def row_lse_of(score_list, flag_list):
    row_max = jnp.full((score_list[0].shape[0],), LOWEST, jnp.float32)
    for block_scores, linked_now in zip(score_list, flag_list):
        row_max = jnp.maximum(row_max, jnp.where(linked_now, jnp.max(block_scores, axis=1), LOWEST))
    row_sum = jnp.zeros_like(row_max)
    for block_scores, linked_now in zip(score_list, flag_list):
        row_sum = row_sum + jnp.where(
            linked_now, jnp.sum(jnp.exp(block_scores - row_max[:, None]), axis=1), 0.0
        )
    return row_max + jnp.log(row_sum)


def column_partial(block_scores, linked_now):
    column_peak = jnp.where(linked_now, jnp.max(block_scores, axis=0), LOWEST)
    column_sum = jnp.where(
        linked_now, jnp.sum(jnp.exp(block_scores - column_peak[None, :]), axis=0), 0.0
    )
    return (column_peak, column_sum)


def merge_columns(partials):
    merged_max = partials[0][0]
    for partial_value in partials[1:]:
        merged_max = jnp.maximum(merged_max, partial_value[0])
    merged_total = jnp.zeros_like(merged_max)
    for partial_value in partials:
        merged_total = merged_total + partial_value[1] * jnp.exp(partial_value[0] - merged_max)
    return merged_max + jnp.log(merged_total)


def grad_weights(block_scores, row_lse, column_lse, linked_now, onehot):
    weight_values = jnp.exp(block_scores - row_lse[:, None]) + jnp.exp(
        block_scores - column_lse[None, :]
    )
    if onehot is not None:
        weight_values = jnp.where(onehot, weight_values - 2.0, weight_values)
    return jnp.where(linked_now, weight_values, 0.0).astype(jnp.bfloat16)


def loss_rows(diagonal_scores, row_lse, column_lse, onehot):
    target = jnp.sum(jnp.where(onehot, diagonal_scores, 0.0), axis=1)
    column_at = jnp.sum(jnp.where(onehot, column_lse[None, :], 0.0), axis=1)
    return row_lse + column_at - 2.0 * target


def per_device(queries, passages, cluster_sizes, positives):
    block_count = lax.axis_size(("pb", "pa"))
    own_index = lax.axis_index(("pb", "pa"))
    block_rows = queries.shape[0]
    reach_most = KMAX - 1
    offsets = list(range(-reach_most, reach_most + 1))
    cluster_of = cluster_index(cluster_sizes, block_count)
    link_flags = {}
    for offset in offsets:
        link_flags[offset] = linked(cluster_of, own_index, own_index - offset)
    onehot = positives[0][:, None] == jnp.arange(block_rows, dtype=jnp.int32)[None, :]
    grad_rows = jnp.zeros(queries.shape, jnp.float32)
    grad_columns = jnp.zeros(passages.shape, jnp.float32)
    neighbors = {0: passages}
    for offset in offsets:
        if offset != 0:
            neighbors[offset] = from_behind(passages, ("pb", "pa"), offset)
    score_blocks = {}
    for offset in offsets:
        score_blocks[offset] = masked_scores(link_flags[offset], queries, neighbors[offset])
    row_lse = row_lse_of(
        [score_blocks[offset] for offset in offsets], [link_flags[offset] for offset in offsets]
    )
    partials = [column_partial(score_blocks[0], link_flags[0])]
    for offset in offsets:
        if offset != 0:
            sent_max, sent_sum = column_partial(score_blocks[offset], link_flags[offset])
            arrived_max, arrived_sum = from_behind((sent_max, sent_sum), ("pb", "pa"), -offset)
            linked_back = link_flags[-offset]
            partials.append(
                (
                    jnp.where(linked_back, arrived_max, LOWEST),
                    jnp.where(linked_back, arrived_sum, 0.0),
                )
            )
    column_lse = merge_columns(partials)
    far_lse = {0: column_lse}
    for offset in offsets:
        if offset != 0:
            far_lse[offset] = from_behind(column_lse, ("pb", "pa"), offset)
    for offset in offsets:
        weights = grad_weights(
            score_blocks[offset],
            row_lse,
            far_lse[offset],
            link_flags[offset],
            onehot if offset == 0 else None,
        )
        grad_rows = grad_rows + masked_product(link_flags[offset], weights, neighbors[offset])
        grad_term = masked_transposed(link_flags[offset], weights, queries)
        if offset != 0:
            grad_term = from_behind(grad_term, ("pb", "pa"), -offset)
        grad_columns = grad_columns + lax.optimization_barrier(grad_term).astype(jnp.float32)
    row_loss = loss_rows(score_blocks[0], row_lse, column_lse, onehot)
    return (grad_rows.astype(jnp.bfloat16), grad_columns.astype(jnp.bfloat16), row_loss[None, :])


def solution(mesh):
    placed = (P(("pb", "pa"), None), P(("pb", "pa"), None), P(), P(("pb", "pa"), None))
    return jax.shard_map(
        per_device,
        mesh=mesh,
        in_specs=placed,
        out_specs=(P(("pb", "pa"), None), P(("pb", "pa"), None), P(("pb", "pa"), None)),
        check_vma=False,
    )
```

profile of v0, /device:TPU:24, one launch (start us, length us, event | category | flops | bytes accessed | tf_op | source)
XLA Modules:
  0.0 645.8 jit_solution(12823822158305849055)
XLA Ops:
  4.0 6.4 collective-permute-start.1
  24.7 7.2 %conditional.17 = (f32[512,512]{1,0:T(8,128)S(1)}, f32[512]{0:T(512)}, f32[512]{0:T(512)S(1)}, f32[1,512]{1,0:T(1,128)S(1)}) conditional(s32[]{:T(128)} %convert_element_type.82, () %tuple.123, (bf16[512,4096]{1,0:T(8,128)(2,1)}, bf16[512,4096]{1,0:T(8,128)(2,1)}) %tuple.124), branch_computations={%region_13.14_spmd, %region_14.17_spmd} | conditional | flops 2148269056 | bytes 9445408 | solution.py:44
  24.7 6.5 %fusion.15 = (f32[512]{0:T(512)S(1)}, f32[512]{0:T(512)}, f32[512,512]{1,0:T(8,128)S(1)}) fusion(bf16[512,4096]{1,0:T(8,128)(2,1)} %get-tuple-element.114, bf16[512,4096]{1,0:T(8,128)(2,1)} %get-tuple-element.115), kind=kOutput, calls=%fused_computation.71 | convolution fusion | flops 2148269056 | bytes 9441280 | tf_op jit(solution)/shard_map/cond/branch_1_fun/dot_general | solution.py:36
  31.9 68.0 %collective-permute-done.2 = bf16[512,4096]{1,0:T(8,128)(2,1)} collective-permute-done((bf16[512,4096]{1,0:T(8,128)(2,1)}, bf16[512,4096]{1,0:T(8,128)(2,1)}, u32[]{:S(2)}, u32[]{:S(2)}) %collective-permute-start.2) | collective-permute-done | bytes 4194336 | tf_op jit(solution)/shard_map/ppermute | solution.py:15
  100.7 180.5 %collective-permute-done.1 = bf16[512,4096]{1,0:T(8,128)(2,1)} collective-permute-done((bf16[512,4096]{1,0:T(8,128)(2,1)}, bf16[512,4096]{1,0:T(8,128)(2,1)}, u32[]{:S(2)}, u32[]{:S(2)}) %collective-permute-start.1) | collective-permute-done | bytes 4194336 | tf_op jit(solution)/shard_map/ppermute | solution.py:15
  281.2 7.2 %conditional.16 = (f32[512,512]{1,0:T(8,128)S(1)}, f32[512]{0:T(512)}, f32[512]{0:T(512)S(1)}, f32[1,512]{1,0:T(1,128)S(1)}) conditional(s32[]{:T(128)} %convert_element_type.81, () %tuple.121, (bf16[512,4096]{1,0:T(8,128)(2,1)}, bf16[512,4096]{1,0:T(8,128)(2,1)}) %tuple.122), branch_computations={%region_9.10_spmd, %region_10.13_spmd} | conditional | flops 2148269056 | bytes 9445408 | solution.py:44
  281.2 6.5 %fusion.14 = (f32[512]{0:T(512)S(1)}, f32[512]{0:T(512)}, f32[512,512]{1,0:T(8,128)S(1)}) fusion(bf16[512,4096]{1,0:T(8,128)(2,1)} %get-tuple-element.112, bf16[512,4096]{1,0:T(8,128)(2,1)} %get-tuple-element.113), kind=kOutput, calls=%fused_computation.70 | convolution fusion | flops 2148269056 | bytes 9441280 | tf_op jit(solution)/shard_map/cond/branch_1_fun/dot_general | solution.py:36
  306.5 6.0 collective-permute-start.8
  335.2 6.0 collective-permute-start.15
  354.8 6.4 collective-permute-start.18
  361.2 6.6 %conditional.26 = (bf16[512,4096]{1,0:T(8,128)(2,1)}) conditional(s32[]{:T(128)} %convert_element_type.81, () %tuple.140, (bf16[512,512]{1,0:T(8,128)(2,1)S(1)}, bf16[512,4096]{1,0:T(8,128)(2,1)}) %tuple.213), branch_computations={%region_49.50_spmd, %region_50.51_spmd} | conditional | flops 2149580800 | bytes 8912904 | solution.py:58
  361.2 6.6 %convolution_convert_fusion.1 = bf16[512,4096]{1,0:T(8,128)(2,1)} fusion(bf16[512,512]{1,0:T(8,128)(2,1)S(1)} %get-tuple-element.132, bf16[512,4096]{1,0:T(8,128)(2,1)} %get-tuple-element.133), kind=kOutput, calls=%fused_computation.6 | convolution fusion | flops 2149580800 | bytes 8912896 | tf_op jit(solution)/shard_map/cond/branch_1_fun/dot_general | solution.py:60
  372.4 11.2 %collective-permute-start.16 = (bf16[512,4096]{1,0:T(8,128)(2,1)}, bf16[512,4096]{1,0:T(8,128)(2,1)}, u32[]{:S(2)}, u32[]{:S(2)}) collective-permute-start(bf16[512,4096]{1,0:T(8,128)(2,1)} %get-tuple-element.275), channel_id=1, source_target_pairs={{0,2},{1,3},{2,4},{3,5},{4,6},{5,7},{6,8},{7,9},{8,10},{9,11},{10,... | collective-permute-start | bytes 12582920 | tf_op jit(solution)/shard_map/ppermute | solution.py:15
  383.6 6.5 %conditional.27 = (bf16[512,4096]{1,0:T(8,128)(2,1)}) conditional(s32[]{:T(128)} %convert_element_type.82, () %tuple.142, (bf16[512,512]{1,0:T(8,128)(2,1)S(1)}, bf16[512,4096]{1,0:T(8,128)(2,1)}) %tuple.217), branch_computations={%region_51.52_spmd, %region_52.53_spmd} | conditional | flops 2149580800 | bytes 8912904 | solution.py:58
  383.7 6.5 %convolution_convert_fusion.2 = bf16[512,4096]{1,0:T(8,128)(2,1)} fusion(bf16[512,512]{1,0:T(8,128)(2,1)S(1)} %get-tuple-element.134, bf16[512,4096]{1,0:T(8,128)(2,1)} %get-tuple-element.135), kind=kOutput, calls=%fused_computation.7 | convolution fusion | flops 2149580800 | bytes 8912896 | tf_op jit(solution)/shard_map/cond/branch_1_fun/dot_general | solution.py:60
  398.7 7.8 %conditional.22 = (f32[512,4096]{1,0:T(8,128)}) conditional(s32[]{:T(128)} %convert_element_type.82, () %tuple.132, (bf16[512,512]{1,0:T(8,128)(2,1)S(1)}, bf16[512,4096]{1,0:T(8,128)(2,1)}) %tuple.218), branch_computations={%region_41.42_spmd, %region_42.43_spmd} | conditional | flops 2147483648 | bytes 13107208 | solution.py:49
  398.7 7.8 %fusion.21 = f32[512,4096]{1,0:T(8,128)} fusion(bf16[512,512]{1,0:T(8,128)(2,1)S(1)} %get-tuple-element.124, bf16[512,4096]{1,0:T(8,128)(2,1)} %get-tuple-element.125), kind=kOutput, calls=%fused_computation.77 | convolution fusion | flops 2147483648 | bytes 13107200 | tf_op jit(solution)/shard_map/cond/branch_1_fun/dot_general | solution.py:51
  410.9 7.8 %conditional.21 = (f32[512,4096]{1,0:T(8,128)}) conditional(s32[]{:T(128)} %convert_element_type.81, () %tuple.130, (bf16[512,512]{1,0:T(8,128)(2,1)S(1)}, bf16[512,4096]{1,0:T(8,128)(2,1)}) %tuple.214), branch_computations={%region_39.40_spmd, %region_40.41_spmd} | conditional | flops 2147483648 | bytes 13107208 | solution.py:49
  410.9 7.7 %fusion.20 = f32[512,4096]{1,0:T(8,128)} fusion(bf16[512,512]{1,0:T(8,128)(2,1)S(1)} %get-tuple-element.122, bf16[512,4096]{1,0:T(8,128)(2,1)} %get-tuple-element.123), kind=kOutput, calls=%fused_computation.76 | convolution fusion | flops 2147483648 | bytes 13107200 | tf_op jit(solution)/shard_map/cond/branch_1_fun/dot_general | solution.py:51
  419.3 17.0 %add_convert_fusion.1 = bf16[512,4096]{1,0:T(8,128)(2,1)} fusion(f32[512,4096]{1,0:T(8,128)} %get-tuple-element.274, f32[512,4096]{1,0:T(8,128)} %get-tuple-element.273, f32[512,4096]{1,0:T(8,128)} %get-tuple-element.272, f32[512,4096]{1,0:T(8,128)} %get-tuple-element.270, f32[512,4096]{1,0:T(8,128)} %get-tuple-element.271), kind=kLoop, calls=%fused_computation.11 | loop fusion | flops 10485760 | bytes 46137344 | tf_op jit(solution)/shard_map/convert_element_type | solution.py:166
  436.3 9.4 %collective-permute-done.19 = bf16[512,4096]{1,0:T(8,128)(2,1)} collective-permute-done((bf16[512,4096]{1,0:T(8,128)(2,1)}, bf16[512,4096]{1,0:T(8,128)(2,1)}, u32[]{:S(2)}, u32[]{:S(2)}) %collective-permute-start.19) | collective-permute-done | bytes 4194336 | tf_op jit(solution)/shard_map/ppermute | solution.py:15
  445.7 93.0 %collective-permute-done.18 = bf16[512,4096]{1,0:T(8,128)(2,1)} collective-permute-done((bf16[512,4096]{1,0:T(8,128)(2,1)}, bf16[512,4096]{1,0:T(8,128)(2,1)}, u32[]{:S(2)}, u32[]{:S(2)}) %collective-permute-start.18) | collective-permute-done | bytes 4194336 | tf_op jit(solution)/shard_map/ppermute | solution.py:15
  538.7 97.7 %collective-permute-done.17 = bf16[512,4096]{1,0:T(8,128)(2,1)} collective-permute-done((bf16[512,4096]{1,0:T(8,128)(2,1)}, bf16[512,4096]{1,0:T(8,128)(2,1)}, u32[]{:S(2)}, u32[]{:S(2)}) %collective-permute-start.17) | collective-permute-done | bytes 4194336 | tf_op jit(solution)/shard_map/ppermute | solution.py:15
  636.4 9.0 %add_convert_fusion = bf16[512,4096]{1,0:T(8,128)(2,1)} fusion(bf16[512,4096]{1,0:T(8,128)(2,1)} %collective-permute-done.19, bf16[512,4096]{1,0:T(8,128)(2,1)} %collective-permute-done.18, bf16[512,4096]{1,0:T(8,128)(2,1)S(1)} %copy-done, bf16[512,4096]{1,0:T(8,128)(2,1)} %collective-permute-done.17, bf16[512,4096]{1,0:T(8,128)(2,1)} %collective-permute-done.16), kind=kLoop, calls=%fused_computation.10 | loop fusion | flops 20971520 | bytes 25165824 | tf_op jit(solution)/shard_map/convert_element_type | solution.py:166
  (98 shorter events, 109.2 us)
Async XLA Ops:
  0.6 99.3 %collective-permute-start.2 = (bf16[512,4096]{1,0:T(8,128)(2,1)}, bf16[512,4096]{1,0:T(8,128)(2,1)}, u32[]{:S(2)}, u32[]{:S(2)}) collective-permute-start(bf16[512,4096]{1,0:T(8,128)(2,1)} %param.35), channel_id=1, source_target_pairs={{0,1},{1,2},{2,3},{3,4},{4,5},{5,6},{6,7},{7,8},{8,9},{9,10},{10,1... | collective-permute-start | bytes 12582920 | tf_op jit(solution)/shard_map/ppermute | solution.py:15
  4.0 277.1 %collective-permute-start.1 = (bf16[512,4096]{1,0:T(8,128)(2,1)}, bf16[512,4096]{1,0:T(8,128)(2,1)}, u32[]{:S(2)}, u32[]{:S(2)}) collective-permute-start(bf16[512,4096]{1,0:T(8,128)(2,1)} %param.35), channel_id=1, source_target_pairs={{1,0},{2,1},{3,2},{4,3},{5,4},{6,5},{7,6},{8,7},{9,8},{10,9},{11,1... | collective-permute-start | bytes 12582920 | tf_op jit(solution)/shard_map/ppermute | solution.py:15
  10.4 277.9 %collective-permute-start = (bf16[512,4096]{1,0:T(8,128)(2,1)}, bf16[512,4096]{1,0:T(8,128)(2,1)}, u32[]{:S(2)}, u32[]{:S(2)}) collective-permute-start(bf16[512,4096]{1,0:T(8,128)(2,1)} %param.35), channel_id=1, source_target_pairs={{2,0},{3,1},{4,2},{5,3},{6,4},{7,5},{8,6},{9,7},{10,8},{11,9},{12,... | collective-permute-start | bytes 12582920 | tf_op jit(solution)/shard_map/ppermute | solution.py:15
  14.0 275.1 %collective-permute-start.3 = (bf16[512,4096]{1,0:T(8,128)(2,1)}, bf16[512,4096]{1,0:T(8,128)(2,1)}, u32[]{:S(2)}, u32[]{:S(2)}) collective-permute-start(bf16[512,4096]{1,0:T(8,128)(2,1)} %param.35), channel_id=1, source_target_pairs={{0,2},{1,3},{2,4},{3,5},{4,6},{5,7},{6,8},{7,9},{8,10},{9,11},{10,... | collective-permute-start | bytes 12582920 | tf_op jit(solution)/shard_map/ppermute | solution.py:15
  290.8 53.9 %copy-start.2 = (f32[512,512]{1,0:T(8,128)S(1)}, f32[512,512]{1,0:T(8,128)}, u32[]{:S(2)}) copy-start(f32[512,512]{1,0:T(8,128)} %copy-done.1) | copy-start | bytes 3145732
  290.8 32.1 %collective-permute-start.7 = (f32[512]{0:T(512)S(1)}, f32[512]{0:T(512)S(1)}, u32[]{:S(2)}, u32[]{:S(2)}) collective-permute-start(f32[512]{0:T(512)S(1)} %broadcast_select_fusion.11), channel_id=1, source_target_pairs={{2,0},{3,1},{4,2},{5,3},{6,4},{7,5},{8,6},{9,7},{10,8},{11,9},{12,... | collective-permute-start | bytes 6152 | tf_op jit(solution)/shard_map/ppermute | solution.py:15
  292.8 30.0 %collective-permute-start.6 = (f32[512]{0:T(512)S(1)}, f32[512]{0:T(512)S(1)}, u32[]{:S(2)}, u32[]{:S(2)}) collective-permute-start(f32[512]{0:T(512)S(1)} %broadcast_select_fusion.10), channel_id=1, source_target_pairs={{1,0},{2,1},{3,2},{4,3},{5,4},{6,5},{7,6},{8,7},{9,8},{10,9},{11,1... | collective-permute-start | bytes 6152 | tf_op jit(solution)/shard_map/ppermute | solution.py:15
  298.7 7.8 %collective-permute-start.11 = (f32[512]{0:T(512)S(1)}, f32[512]{0:T(512)S(1)}, u32[]{:S(2)}, u32[]{:S(2)}) collective-permute-start(f32[512]{0:T(512)S(1)} %broadcast_select_fusion.6), channel_id=1, source_target_pairs={{2,0},{3,1},{4,2},{5,3},{6,4},{7,5},{8,6},{9,7},{10,8},{11,9},{12,... | collective-permute-start | bytes 6152 | tf_op jit(solution)/shard_map/ppermute | solution.py:15
  300.6 11.9 %collective-permute-start.10 = (f32[512]{0:T(512)S(1)}, f32[512]{0:T(512)S(1)}, u32[]{:S(2)}, u32[]{:S(2)}) collective-permute-start(f32[512]{0:T(512)S(1)} %broadcast_select_fusion.5), channel_id=1, source_target_pairs={{1,0},{2,1},{3,2},{4,3},{5,4},{6,5},{7,6},{8,7},{9,8},{10,9},{11,1... | collective-permute-start | bytes 6152 | tf_op jit(solution)/shard_map/ppermute | solution.py:15
  302.6 15.4 %collective-permute-start.9 = (f32[512]{0:T(512)S(1)}, f32[512]{0:T(512)S(1)}, u32[]{:S(2)}, u32[]{:S(2)}) collective-permute-start(f32[512]{0:T(512)S(1)} %broadcast_select_fusion.7), channel_id=1, source_target_pairs={{0,1},{1,2},{2,3},{3,4},{4,5},{5,6},{6,7},{7,8},{8,9},{9,10},{10,1... | collective-permute-start | bytes 6152 | tf_op jit(solution)/shard_map/ppermute | solution.py:15
  306.5 16.3 %collective-permute-start.8 = (f32[512]{0:T(512)S(1)}, f32[512]{0:T(512)S(1)}, u32[]{:S(2)}, u32[]{:S(2)}) collective-permute-start(f32[512]{0:T(512)S(1)} %broadcast_select_fusion.8), channel_id=1, source_target_pairs={{0,2},{1,3},{2,4},{3,5},{4,6},{5,7},{6,8},{7,9},{8,10},{9,11},{10,... | collective-permute-start | bytes 6152 | tf_op jit(solution)/shard_map/ppermute | solution.py:15
  312.6 10.3 %collective-permute-start.5 = (f32[512]{0:T(512)S(1)}, f32[512]{0:T(512)S(1)}, u32[]{:S(2)}, u32[]{:S(2)}) collective-permute-start(f32[512]{0:T(512)S(1)} %broadcast_select_fusion.12), channel_id=1, source_target_pairs={{0,1},{1,2},{2,3},{3,4},{4,5},{5,6},{6,7},{7,8},{8,9},{9,10},{10,1... | collective-permute-start | bytes 6152 | tf_op jit(solution)/shard_map/ppermute | solution.py:15
  318.0 9.4 %collective-permute-start.4 = (f32[512]{0:T(512)S(1)}, f32[512]{0:T(512)S(1)}, u32[]{:S(2)}, u32[]{:S(2)}) collective-permute-start(f32[512]{0:T(512)S(1)} %broadcast_select_fusion.13), channel_id=1, source_target_pairs={{0,2},{1,3},{2,4},{3,5},{4,6},{5,7},{6,8},{7,9},{8,10},{9,11},{10,... | collective-permute-start | bytes 6152 | tf_op jit(solution)/shard_map/ppermute | solution.py:15
  327.5 13.8 %collective-permute-start.13 = (f32[512]{0:T(512)S(1)}, f32[512]{0:T(512)S(1)}, u32[]{:S(2)}, u32[]{:S(2)}) collective-permute-start(f32[512]{0:T(512)S(1)} %log_add_fusion), channel_id=1, source_target_pairs={{1,0},{2,1},{3,2},{4,3},{5,4},{6,5},{7,6},{8,7},{9,8},{10,9},{11,1... | collective-permute-start | bytes 6152 | tf_op jit(solution)/shard_map/ppermute | solution.py:15
  329.4 11.9 %collective-permute-start.12 = (f32[512]{0:T(512)S(1)}, f32[512]{0:T(512)S(1)}, u32[]{:S(2)}, u32[]{:S(2)}) collective-permute-start(f32[512]{0:T(512)S(1)} %log_add_fusion), channel_id=1, source_target_pairs={{2,0},{3,1},{4,2},{5,3},{6,4},{7,5},{8,6},{9,7},{10,8},{11,9},{12,... | collective-permute-start | bytes 6152 | tf_op jit(solution)/shard_map/ppermute | solution.py:15
  331.3 10.0 %collective-permute-start.14 = (f32[512]{0:T(512)S(1)}, f32[512]{0:T(512)S(1)}, u32[]{:S(2)}, u32[]{:S(2)}) collective-permute-start(f32[512]{0:T(512)S(1)} %log_add_fusion), channel_id=1, source_target_pairs={{0,1},{1,2},{2,3},{3,4},{4,5},{5,6},{6,7},{7,8},{8,9},{9,10},{10,1... | collective-permute-start | bytes 6152 | tf_op jit(solution)/shard_map/ppermute | solution.py:15
  335.2 9.4 %collective-permute-start.15 = (f32[512]{0:T(512)S(1)}, f32[512]{0:T(512)S(1)}, u32[]{:S(2)}, u32[]{:S(2)}) collective-permute-start(f32[512]{0:T(512)S(1)} %log_add_fusion), channel_id=1, source_target_pairs={{0,2},{1,3},{2,4},{3,5},{4,6},{5,7},{6,8},{7,9},{8,10},{9,11},{10,... | collective-permute-start | bytes 6152 | tf_op jit(solution)/shard_map/ppermute | solution.py:15
  350.4 95.3 %collective-permute-start.19 = (bf16[512,4096]{1,0:T(8,128)(2,1)}, bf16[512,4096]{1,0:T(8,128)(2,1)}, u32[]{:S(2)}, u32[]{:S(2)}) collective-permute-start(bf16[512,4096]{1,0:T(8,128)(2,1)} %get-tuple-element.279), channel_id=1, source_target_pairs={{2,0},{3,1},{4,2},{5,3},{6,4},{7,5},{8,6},{9,7},{10,8},{11,9},{12,... | collective-permute-start | bytes 12582920 | tf_op jit(solution)/shard_map/ppermute | solution.py:15
  352.3 8.9 %copy-start.3 = (bf16[512,512]{1,0:T(8,128)(2,1)S(1)}, bf16[512,512]{1,0:T(8,128)(2,1)}, u32[]{:S(2)}) copy-start(bf16[512,512]{1,0:T(8,128)(2,1)} %get-tuple-element.226) | copy-start | bytes 1572868
  354.8 183.9 %collective-permute-start.18 = (bf16[512,4096]{1,0:T(8,128)(2,1)}, bf16[512,4096]{1,0:T(8,128)(2,1)}, u32[]{:S(2)}, u32[]{:S(2)}) collective-permute-start(bf16[512,4096]{1,0:T(8,128)(2,1)} %get-tuple-element.278), channel_id=1, source_target_pairs={{1,0},{2,1},{3,2},{4,3},{5,4},{6,5},{7,6},{8,7},{9,8},{10,9},{11,1... | collective-permute-start | bytes 12582920 | tf_op jit(solution)/shard_map/ppermute | solution.py:15
  367.8 268.6 %collective-permute-start.17 = (bf16[512,4096]{1,0:T(8,128)(2,1)}, bf16[512,4096]{1,0:T(8,128)(2,1)}, u32[]{:S(2)}, u32[]{:S(2)}) collective-permute-start(bf16[512,4096]{1,0:T(8,128)(2,1)} %get-tuple-element.276), channel_id=1, source_target_pairs={{0,1},{1,2},{2,3},{3,4},{4,5},{5,6},{6,7},{7,8},{8,9},{9,10},{10,1... | collective-permute-start | bytes 12582920 | tf_op jit(solution)/shard_map/ppermute | solution.py:15
  369.8 13.9 %copy-start.5 = (bf16[512,512]{1,0:T(8,128)(2,1)S(1)}, bf16[512,512]{1,0:T(8,128)(2,1)}, u32[]{:S(2)}) copy-start(bf16[512,512]{1,0:T(8,128)(2,1)} %get-tuple-element.225) | copy-start | bytes 1572868
  372.4 264.0 %collective-permute-start.16 = (bf16[512,4096]{1,0:T(8,128)(2,1)}, bf16[512,4096]{1,0:T(8,128)(2,1)}, u32[]{:S(2)}, u32[]{:S(2)}) collective-permute-start(bf16[512,4096]{1,0:T(8,128)(2,1)} %get-tuple-element.275), channel_id=1, source_target_pairs={{0,2},{1,3},{2,4},{3,5},{4,6},{5,7},{6,8},{7,9},{8,10},{9,11},{10,... | collective-permute-start | bytes 12582920 | tf_op jit(solution)/shard_map/ppermute | solution.py:15
  419.3 217.1 %copy-start = (bf16[512,4096]{1,0:T(8,128)(2,1)S(1)}, bf16[512,4096]{1,0:T(8,128)(2,1)}, u32[]{:S(2)}) copy-start(bf16[512,4096]{1,0:T(8,128)(2,1)} %get-tuple-element.277) | copy-start | bytes 12582916
  (5 other events, 27.1 us)
where the time goes:
time: 655 us; the launch traced here: 646 us
  waiting for transfers between devices  457 us (70%)
  starting transfers between devices  80.5 us (12%)
  matrix products  41.6 us (6%)
  other arithmetic  34.6 us (5%)
  local copies, waits for them, and re-layouts  25.3 us (4%)
  between operations  6.59 us (1%)
    ppermute x20, waiting for transfers between devices, from_behind(): return lax.ppermute(x, axis, pairs)  457 us
    ppermute x20, starting transfers between devices, from_behind(): return lax.ppermute(x, axis, pairs)  80.5 us
    another operation x10, local copies, waits for them, and re-layouts  21.2 us
    convert_element_type x1, other arithmetic, per_device(): grad_rows.astype(jnp.bfloat16)  17 us
    dot_general x2, matrix products, masked_product(): jnp.dot(weights, operand, preferred_element_type=jnp.float32)  15.5 us
    dot_general x2, matrix products, masked_transposed(): lax.dot_general(weights, operand, (((0,), (0,)), ((), ())), preferred_ele...  13.1 us
  transfers between devices with their start and end apart: 20, of which 7 were waited for; matrix products, arithmetic and copies ran while one was open for 13% of the time, Pallas kernels for 0%

commit v1 on v0

v1 whole, which is shorter than its diff:
```python
import jax
import jax.numpy as jnp
from jax import lax
from jax.experimental import pallas as pl
from jax.experimental.pallas import tpu as pltpu
from jax.sharding import PartitionSpec as P

BLK = 512
D = 4096
NB = 128
NCL = 64
NC = 8
CW = D // NC
PA = 16
HALVES = 2
VM = 62
HB = BLK // HALVES
LOWEST = -1e30
SCALE = float(D) ** (-0.5)
F32 = jnp.float32
BF16 = jnp.bfloat16
MESH = pl.DeviceIdType.MESH


def dot_nt(a, b):
    return lax.dot_general(a, b, (((1,), (1,)), ((), ())), preferred_element_type=F32)


def dot_nn(a, b):
    return jnp.dot(a, b, preferred_element_type=F32)


def mask_of(flag, shape):
    return jnp.full(shape, flag, jnp.int32) > 0


def exchange_kernel(
    sizes_ref, pos_ref, q_hbm, p_hbm,
    gq_hbm, gp_hbm, loss_ref,
    q0, p0, pl_in, pr_in, xl_in, xr_in, tl_in, tr_in, send_r, send_l,
    s3, row_lse, col_lse, msg_l, msg_r, pos_t, w_row, wt_p, stage,
    sem_q, sem_p, ps_r, ps_l, pr_r, pr_l, xs_r, xs_l, xr_r, xr_l, ts_r, ts_l, tr_r, tr_l,
    msg_send, msg_recv, out_sem,
):
    pb, pa = lax.axis_index("pb"), lax.axis_index("pa")
    me = pb * PA + pa
    after = lax.rem(me + 1, NB)
    before = lax.rem(me + NB - 1, NB)
    right = (after // PA, lax.rem(after, PA))
    left = (before // PA, lax.rem(before, PA))

    barrier = pltpu.get_barrier_semaphore()
    for neighbour in (left, right):
        pl.semaphore_signal(barrier, inc=1, device_id=neighbour, device_id_type=MESH)
    pl.semaphore_wait(barrier, 2)

    def columns(c):
        return pl.ds(pl.multiple_of(c * CW, CW), CW)

    def remote(src, dst, send, recv, to):
        return pltpu.make_async_remote_copy(
            src_ref=src, dst_ref=dst, send_sem=send, recv_sem=recv, device_id=to, device_id_type=MESH
        )

    def p_right(c):
        return remote(p_hbm.at[:, columns(c)], pl_in.at[c], ps_r.at[c], pr_r.at[c], right)

    def p_left(c):
        return remote(p_hbm.at[:, columns(c)], pr_in.at[c], ps_l.at[c], pr_l.at[c], left)

    def x_right(c):
        return remote(send_r.at[c], xl_in.at[c], xs_r.at[c], xr_r.at[c], right)

    def x_left(c):
        return remote(send_l.at[c], xr_in.at[c], xs_l.at[c], xr_l.at[c], left)

    def t_right(c):
        return remote(send_r.at[c], tl_in.at[c], ts_r.at[c], tr_r.at[c], right)

    def t_left(c):
        return remote(send_l.at[c], tr_in.at[c], ts_l.at[c], tr_l.at[c], left)

    def q_load(c):
        return pltpu.make_async_copy(q_hbm.at[:, columns(c)], q0.at[c], sem_q.at[c])

    def p_load(c):
        return pltpu.make_async_copy(p_hbm.at[:, columns(c)], p0.at[c], sem_p.at[c])

    @pl.loop(0, NC)
    def _(c):
        p_right(c).start()
        p_left(c).start()
        q_load(c).start()
        p_load(c).start()

    def scan_sizes(k, carry):
        end, at_me, at_next, at_before, at_after = carry
        end = end + sizes_ref[k]
        one = jnp.int32(1)
        return (
            end,
            jnp.where(end == me, one, at_me),
            jnp.where(end == me + 1, one, at_next),
            jnp.where(end == me - 1, one, at_before),
            jnp.where(end == me + 2, one, at_after),
        )

    zero = jnp.int32(0)
    _, at_me, at_next, at_before, at_after = lax.fori_loop(0, NCL, scan_sizes, (zero,) * 5)
    has_l = jnp.where(me > 0, 1 - at_me, 0)
    has_r = jnp.where(me < NB - 1, 1 - at_next, 0)
    far_l = jnp.where(me > 1, 1 - at_before, 0) * has_l
    far_r = jnp.where(me < NB - 2, 1 - at_after, 0) * has_r
    rows_l = has_l - far_l
    rows_r = has_r - far_r

    def add_scores(r, k, c, a_ref, b_ref):
        for h in range(HALVES):
            ref = s3.at[pl.ds(r * BLK + h * HB, HB), pl.ds(k * BLK, BLK)]
            part = dot_nt(a_ref[c, h * HB:(h + 1) * HB, :], b_ref[c])

            @pl.when(c == 0)
            def _():
                ref[...] = part

            @pl.when(c > 0)
            def _():
                ref[...] += part

    @pl.loop(0, NC)
    def _(c):
        q_load(c).wait()
        p_load(c).wait()
        add_scores(1, 1, c, q0, p0)

    @pl.loop(0, NC)
    def _(c):
        p_right(c).wait_recv()
        p_left(c).wait_recv()
        for h in range(HALVES):
            here = slice(h * HB, (h + 1) * HB)
            send_r[c, here, :] = jnp.where(mask_of(has_l, (HB, CW)), pl_in[c, here, :], q0[c, here, :])
        x_right(c).start()
        for h in range(HALVES):
            here = slice(h * HB, (h + 1) * HB)
            send_l[c, here, :] = jnp.where(mask_of(has_r, (HB, CW)), pr_in[c, here, :], q0[c, here, :])
        x_left(c).start()
        add_scores(1, 0, c, q0, pl_in)
        add_scores(1, 2, c, q0, pr_in)

    @pl.loop(0, NC)
    def _(c):
        x_right(c).wait_recv()
        x_left(c).wait_recv()
        for r, x_in in ((0, xl_in), (2, xr_in)):
            for k, p_in in ((0, pl_in), (1, p0), (2, pr_in)):
                add_scores(r, k, c, x_in, p_in)

    held_rows = (rows_l, jnp.int32(1), rows_r)
    held_cols = (has_l, jnp.int32(1), has_r)
    RT = 64

    def valid(r, k, shape):
        return mask_of(held_rows[r] * held_cols[k], shape)

    col_peak = [jnp.full((8, BLK), LOWEST, F32) for _ in range(3)]
    for r in range(3):
        def peaks(t, peak):
            rows = pl.ds(pl.multiple_of(r * BLK + t * RT, RT), RT)
            tiles = [
                jnp.where(valid(r, k, (RT, BLK)), s3[rows, k * BLK:(k + 1) * BLK] * SCALE, LOWEST)
                for k in range(3)
            ]
            top = jnp.max(jnp.maximum(jnp.maximum(tiles[0], tiles[1]), tiles[2]), axis=1, keepdims=True)
            total = jnp.zeros((RT, 1), F32)
            for tile in tiles:
                total = total + jnp.sum(jnp.exp(tile - top), axis=1, keepdims=True)
            row_lse[rows, :] = jnp.broadcast_to(top + jnp.log(total), (RT, 128))
            return tuple(
                jnp.maximum(old, jnp.max(tile.reshape(RT // 8, 8, BLK), axis=0))
                for old, tile in zip(peak, tiles)
            )

        col_peak = lax.fori_loop(0, BLK // RT, peaks, tuple(col_peak))
    col_top = [jnp.max(peak, axis=0, keepdims=True) for peak in col_peak]
    col_sum = [jnp.zeros((8, BLK), F32) for _ in range(3)]
    for r in range(3):
        def sums(t, total):
            rows = pl.ds(pl.multiple_of(r * BLK + t * RT, RT), RT)
            out = []
            for k in range(3):
                tile = jnp.where(valid(r, k, (RT, BLK)), s3[rows, k * BLK:(k + 1) * BLK] * SCALE, LOWEST)
                part = jnp.exp(tile - col_top[k])
                out.append(total[k] + jnp.sum(part.reshape(RT // 8, 8, BLK), axis=0))
            return tuple(out)

        col_sum = lax.fori_loop(0, BLK // RT, sums, tuple(col_sum))
    for k in range(3):
        lse = col_top[k] + jnp.log(jnp.sum(col_sum[k], axis=0, keepdims=True))
        col_lse[:, k * BLK:(k + 1) * BLK] = jnp.broadcast_to(lse, (8, BLK))

    tell_r = remote(col_lse, msg_l, msg_send.at[0], msg_recv.at[0], right)
    tell_l = remote(col_lse, msg_r, msg_send.at[1], msg_recv.at[1], left)
    tell_r.start()
    tell_l.start()

    def weight_tile(tile, lse_rows, lse_cols):
        return jnp.exp(tile - lse_rows) + jnp.exp(tile - lse_cols)

    def weights_t(r, k, out, at):
        ok = held_rows[r] * held_cols[k]
        lse_cols = col_lse[0:1, k * BLK:(k + 1) * BLK]

        @pl.loop(0, 4)
        def _(t):
            rows = pl.ds(pl.multiple_of(r * BLK + t * 128, 128), 128)
            tile = s3[rows, k * BLK:(k + 1) * BLK] * SCALE
            value = weight_tile(tile, row_lse[rows, 0:1], lse_cols)
            value = jnp.where(mask_of(ok, value.shape), value, 0.0)
            out[:, pl.ds(pl.multiple_of(at + t * 128, 128), 128)] = value.T.astype(BF16)

    for place, (r, k) in enumerate(((1, 0), (2, 0), (1, 2), (0, 2))):
        weights_t(r, k, w_row, place * BLK)

    @pl.loop(0, NC)
    def _(c):
        x_left(c).wait_send()
        for h in range(HALVES):
            here = slice(h * HB, (h + 1) * HB)
            term = dot_nn(w_row[here, :BLK], q0[c]) + dot_nn(w_row[here, BLK:2 * BLK], xr_in[c])
            send_l[c, here, :] = term.astype(BF16)
        t_left(c).start()
        x_right(c).wait_send()
        for h in range(HALVES):
            here = slice(h * HB, (h + 1) * HB)
            term = dot_nn(w_row[here, 2 * BLK:3 * BLK], q0[c]) + dot_nn(w_row[here, 3 * BLK:], xl_in[c])
            send_r[c, here, :] = term.astype(BF16)
        t_right(c).start()

    @pl.loop(0, NC)
    def _(c):
        for h in range(HALVES):
            here = slice(h * HB, (h + 1) * HB)
            xl_in[c, here, :] = jnp.where(mask_of(far_r, (HB, CW)), xr_in[c, here, :], xl_in[c, here, :])
        add_scores(0, 0, c, q0, xl_in)

    tell_r.wait()
    tell_l.wait()
    end = far_l + far_r

    def pick(from_left, from_right, own):
        out = own
        if from_left is not None:
            out = jnp.where(mask_of(far_l, (1, BLK)), msg_l[0:1, from_left * BLK:(from_left + 1) * BLK], out)
        if from_right is not None:
            out = jnp.where(mask_of(far_r, (1, BLK)), msg_r[0:1, from_right * BLK:(from_right + 1) * BLK], out)
        return out

    own_cols = [col_lse[0:1, k * BLK:(k + 1) * BLK] for k in range(3)]
    lse_l = pick(1, None, own_cols[0])
    lse_0 = pick(2, 0, own_cols[1])
    lse_r = pick(None, 1, own_cols[2])
    lse_x = pick(0, 2, own_cols[0])
    pos_t[...] = jnp.broadcast_to(pos_ref[...].astype(F32), (128, BLK)).T
    flags = (has_l, jnp.int32(1), has_r, end)
    WT = 128

    @pl.loop(0, BLK // WT)
    def _(t):
        here = pl.ds(pl.multiple_of(t * WT, WT), WT)
        own = pl.ds(pl.multiple_of(BLK + t * WT, WT), WT)
        shape = (WT, BLK)
        raw = [s3[own, k * BLK:(k + 1) * BLK] * SCALE for k in range(3)] + [s3[here, :BLK] * SCALE]
        tiles = [jnp.where(mask_of(flag, shape), tile, LOWEST) for flag, tile in zip(flags, raw)]
        top = jnp.max(
            jnp.maximum(jnp.maximum(tiles[0], tiles[1]), jnp.maximum(tiles[2], tiles[3])), axis=1, keepdims=True
        )
        total = jnp.zeros((WT, 1), F32)
        for tile in tiles:
            total = total + jnp.sum(jnp.exp(tile - top), axis=1, keepdims=True)
        lse_rows = top + jnp.log(total)
        lane = lax.broadcasted_iota(jnp.int32, shape, 1).astype(F32)
        onehot = jnp.concatenate([pos_t[here, :]] * 4, axis=1) == lane
        hits = jnp.where(onehot, lse_0 - 2.0 * raw[1], 0.0)
        loss = lse_rows + jnp.sum(hits, axis=1, keepdims=True)
        loss_ref[:, here] = jnp.broadcast_to(loss, (WT, 128)).T[0:1, :]
        for k, (flag, tile, lse_cols) in enumerate(zip(flags, raw, (lse_l, lse_0, lse_r, lse_x))):
            value = weight_tile(tile, lse_rows, lse_cols)
            if k == 1:
                value = jnp.where(onehot, value - 2.0, value)
            value = jnp.where(mask_of(flag, shape), value, 0.0)
            w_row[here, k * BLK:(k + 1) * BLK] = value.astype(BF16)
            if k == 1:
                wt_p[:, here] = value.T.astype(BF16)

    weights_t(0, 1, wt_p, BLK)
    weights_t(2, 1, wt_p, 2 * BLK)

    def gq_out(c, slot):
        return pltpu.make_async_copy(stage.at[slot], gq_hbm.at[:, columns(c)], out_sem.at[slot])

    def gp_out(c, slot):
        return pltpu.make_async_copy(stage.at[slot], gp_hbm.at[:, columns(c)], out_sem.at[slot])

    @pl.loop(0, NC)
    def _(c):
        slot = lax.rem(c, 2)

        @pl.when(c >= 2)
        def _():
            gq_out(c - 2, slot).wait()

        for h in range(HALVES):
            here = slice(h * HB, (h + 1) * HB)
            total = dot_nn(w_row[here, :BLK], pl_in[c]) + dot_nn(w_row[here, BLK:2 * BLK], p0[c])
            total = total + dot_nn(w_row[here, 2 * BLK:3 * BLK], pr_in[c]) + dot_nn(w_row[here, 3 * BLK:], xl_in[c])
            stage[slot, here, :] = total.astype(BF16)
        gq_out(c, slot).start()

    @pl.loop(0, NC)
    def _(c):
        slot = lax.rem(c, 2)

        @pl.when(c < 2)
        def _():
            gq_out(NC - 2 + c, slot).wait()

        @pl.when(c >= 2)
        def _():
            gp_out(c - 2, slot).wait()

        t_right(c).wait_recv()
        t_left(c).wait_recv()
        shape = (HB, CW)
        for h in range(HALVES):
            here = slice(h * HB, (h + 1) * HB)
            total = dot_nn(wt_p[here, :BLK], q0[c]) + dot_nn(wt_p[here, BLK:2 * BLK], xl_in[c])
            total = total + dot_nn(wt_p[here, 2 * BLK:], xr_in[c])
            total = total + jnp.where(mask_of(far_l, shape), tl_in[c, here, :].astype(F32), 0.0)
            total = total + jnp.where(mask_of(far_r, shape), tr_in[c, here, :].astype(F32), 0.0)
            stage[slot, here, :] = total.astype(BF16)
        gp_out(c, slot).start()

    for c in (NC - 2, NC - 1):
        gp_out(c, c % 2).wait()

    @pl.loop(0, NC)
    def _(c):
        p_right(c).wait_send()
        p_left(c).wait_send()
        t_right(c).wait_send()
        t_left(c).wait_send()


def per_device(queries, passages, cluster_sizes, positives):
    block = pltpu.VMEM((NC, BLK, CW), BF16)
    dma = pltpu.SemaphoreType.DMA
    any_space = pl.BlockSpec(memory_space=pl.ANY)
    in_vmem = pl.BlockSpec(memory_space=pltpu.VMEM)
    return pl.pallas_call(
        exchange_kernel,
        out_shape=(
            jax.ShapeDtypeStruct((BLK, D), BF16),
            jax.ShapeDtypeStruct((BLK, D), BF16),
            jax.ShapeDtypeStruct((1, BLK), F32),
        ),
        in_specs=[pl.BlockSpec(memory_space=pltpu.SMEM), in_vmem, any_space, any_space],
        out_specs=(any_space, any_space, in_vmem),
        scratch_shapes=[block] * 10
        + [
            pltpu.VMEM((3 * BLK, 3 * BLK), F32),
            pltpu.VMEM((3 * BLK, 128), F32),
            pltpu.VMEM((8, 3 * BLK), F32),
            pltpu.VMEM((8, 3 * BLK), F32),
            pltpu.VMEM((8, 3 * BLK), F32),
            pltpu.VMEM((BLK, 128), F32),
            pltpu.VMEM((BLK, 4 * BLK), BF16),
            pltpu.VMEM((BLK, 3 * BLK), BF16),
            pltpu.VMEM((2, BLK, CW), BF16),
        ]
        + [dma((NC,))] * 14
        + [dma((2,))] * 3,
        compiler_params=pltpu.CompilerParams(
            collective_id=0, has_side_effects=True, vmem_limit_bytes=VM * 1024 * 1024
        ),
        cost_estimate=pl.CostEstimate(flops=50_000_000_000, bytes_accessed=64 << 20, transcendentals=0),
    )(cluster_sizes, positives, queries, passages)


def solution(mesh):
    placed = (P(("pb", "pa"), None), P(("pb", "pa"), None), P(), P(("pb", "pa"), None))
    return jax.shard_map(
        per_device,
        mesh=mesh,
        in_specs=placed,
        out_specs=(P(("pb", "pa"), None), P(("pb", "pa"), None), P(("pb", "pa"), None)),
        check_vma=False,
    )
```

time: 655 us -> 315 us (0.48); the launches traced: 646 us -> 314 us
  waiting for transfers between devices: 457 us -> 0 us
  Pallas kernels: 0 us -> 306 us
  starting transfers between devices: 80.5 us -> 0 us
  matrix products: 41.6 us -> 0 us
  other arithmetic: 34.6 us -> 0 us
  local copies, waits for them, and re-layouts: 25.3 us -> 7.45 us
    ppermute x20 -> x0, waiting for transfers between devices: 457 us -> none  [from_behind(): return lax.ppermute(x, axis, pairs)]
    pallas_call x0 -> x1, Pallas kernels: none -> 306 us  [per_device(): pl.pallas_call(exchange_kernel, out_shape=(jax.ShapeDtypeStruct((BLK, D),...]
    ppermute x20 -> x0, starting transfers between devices: 80.5 us -> none  [from_behind(): return lax.ppermute(x, axis, pairs)]
    dot_general x6 -> x0, matrix products: 41.6 us -> none  [the longest x2 15.5 us: masked_product(): jnp.dot(weights, operand, preferred_element_type=jnp.float32)]
    convert_element_type x2 -> x0, other arithmetic: 26 us -> none  [the longest x1 17 us: per_device(): grad_rows.astype(jnp.bfloat16)]
    another operation x10 -> x0, local copies, waits for them, and re-layouts: 21.2 us -> none
    reduce_sum x4 -> x0, other arithmetic: 7.07 us -> none  [the longest x1 3.21 us: loss_rows(): column_at = jnp.sum(jnp.where(onehot, column_lse[None, :], 0.0), axis=1)]
  transfers between devices with their start and end apart: 20 -> 0, of which waited for: 7 -> 0; matrix products, arithmetic and copies ran while one was open for 13% -> 0% of each run, Pallas kernels for 0% -> 0%
where the time goes in v1:
time: 315 us; the launch traced here: 314 us
  Pallas kernels  306 us (97%)
  local copies, waits for them, and re-layouts  7.45 us (2%)
    pallas_call x1, Pallas kernels, per_device(): pl.pallas_call(exchange_kernel, out_shape=(jax.ShapeDtypeStruct((BLK, D),...  306 us
    unnamed x7, local copies, waits for them, and re-layouts  7.45 us

profile of v1, /device:TPU:24, one launch (start us, length us, event | category | flops | bytes accessed | tf_op | source)
XLA Modules:
  0.0 313.7 jit_solution(16286142269636355973)
XLA Ops:
  0.6 305.6 %shard_map.67 = (bf16[512,4096]{1,0:T(8,128)(2,1)}, bf16[512,4096]{1,0:T(8,128)(2,1)}, f32[1,512]{1,0:T(1,128)}) custom-call(s32[64]{0:T(128)} %sizes_ref.1, s32[1,512]{1,0:T(1,128)} %pos_ref.1, bf16[512,4096]{1,0:T(8,128)(2,1)} %q_hbm.1, bf16[512,4096]{1,0:T(8,128)(2,1)} %p_hbm.1), custom_call_target="tpu_custom_call" | custom-call | flops 49999998976 | bytes 67108864 | tf_op jit(solution)/shard_map/pallas_call | solution.py:360
  306.3 0.0 copy-start
  306.3 4.8 %copy.10 = bf16[512,4096]{1,0:T(8,128)(2,1)} copy(bf16[512,4096]{1,0:T(8,128)(2,1)} %get-tuple-element.6) | data formatting | bytes 8388608
  311.1 0.0 copy-done
  311.1 0.0 copy-start.1
  311.2 2.0 copy.11
  313.2 0.0 copy-done.1
  313.2 0.6 copy.12
Async XLA Ops:
  306.3 4.9 %copy-start = (bf16[512,4096]{1,0:T(8,128)(2,1)S(1)}, bf16[512,4096]{1,0:T(8,128)(2,1)}, u32[]{:S(2)}) copy-start(bf16[512,4096]{1,0:T(8,128)(2,1)} %get-tuple-element.7) | copy-start | bytes 12582916
  311.1 2.0 copy-start.1

commit v2 on v1

--- a/solution.py
+++ b/solution.py
@@ -13,6 +13,7 @@
 CW = D // NC
 PA = 16
 HALVES = 2
+HOLD = 6
 VM = 62
 HB = BLK // HALVES
 LOWEST = -1e30
@@ -40,7 +41,7 @@
     q0, p0, pl_in, pr_in, xl_in, xr_in, tl_in, tr_in, send_r, send_l,
     s3, row_lse, col_lse, msg_l, msg_r, pos_t, w_row, wt_p, stage,
     sem_q, sem_p, ps_r, ps_l, pr_r, pr_l, xs_r, xs_l, xr_r, xr_l, ts_r, ts_l, tr_r, tr_l,
-    msg_send, msg_recv, out_sem,
+    msg_send, msg_recv, out_sem, token,
 ):
     pb, pa = lax.axis_index("pb"), lax.axis_index("pa")
     me = pb * PA + pa
@@ -49,10 +50,21 @@
     right = (after // PA, lax.rem(after, PA))
     left = (before // PA, lax.rem(before, PA))
 
+    core = lax.rem(pb, 2)
+    twin = (pb + 1 - 2 * core, pa)
+
     barrier = pltpu.get_barrier_semaphore()
-    for neighbour in (left, right):
+    for neighbour in (left, right, twin):
         pl.semaphore_signal(barrier, inc=1, device_id=neighbour, device_id_type=MESH)
-    pl.semaphore_wait(barrier, 2)
+    pl.semaphore_wait(barrier, 3)
+
+    WAYS = ("r", "l")
+    order = {
+        "r": lax.rem(core + jnp.where(pa == PA - 1, 1, 0), 2),
+        "l": lax.rem(core + jnp.where(pa == 0, 1, 0), 2),
+    }
+    mixed = jnp.logical_or(pa == PA - 1, pa == 0)
+    give_at = jnp.where(mixed, NC - HOLD, NC - 1)
 
     def columns(c):
         return pl.ds(pl.multiple_of(c * CW, CW), CW)
@@ -140,16 +152,42 @@
         for h in range(HALVES):
             here = slice(h * HB, (h + 1) * HB)
             send_r[c, here, :] = jnp.where(mask_of(has_l, (HB, CW)), pl_in[c, here, :], q0[c, here, :])
-        x_right(c).start()
+        @pl.when(jnp.logical_or(order["r"] == 0, c < NC - HOLD))
+        def _():
+            x_right(c).start()
+
         for h in range(HALVES):
             here = slice(h * HB, (h + 1) * HB)
             send_l[c, here, :] = jnp.where(mask_of(has_r, (HB, CW)), pr_in[c, here, :], q0[c, here, :])
-        x_left(c).start()
+        @pl.when(jnp.logical_or(order["l"] == 0, c < NC - HOLD))
+        def _():
+            x_left(c).start()
+
         add_scores(1, 0, c, q0, pl_in)
         add_scores(1, 2, c, q0, pr_in)
 
-    @pl.loop(0, NC)
-    def _(c):
+    send_x = {"r": x_right, "l": x_left}
+
+    @pl.loop(0, NC)
+    def _(c):
+        for at, way in enumerate(WAYS):
+            @pl.when(jnp.logical_and(c == give_at, order[way] == 0))
+            def _():
+                @pl.loop(0, NC - 1)
+                def _(k):
+                    send_x[way](k).wait_send()
+
+                pl.semaphore_signal(token.at[at], inc=1, device_id=twin, device_id_type=MESH)
+
+        for at, way in enumerate(WAYS):
+            @pl.when(jnp.logical_and(c == NC - HOLD, order[way] == 1))
+            def _():
+                pl.semaphore_wait(token.at[at], 1)
+
+                @pl.loop(NC - HOLD, NC)
+                def _(k):
+                    send_x[way](k).start()
+
         x_right(c).wait_recv()
         x_left(c).wait_recv()
         for r, x_in in ((0, xl_in), (2, xr_in)):
@@ -224,13 +262,19 @@
 
     @pl.loop(0, NC)
     def _(c):
-        x_left(c).wait_send()
+        @pl.when(jnp.logical_or(order["l"] == 1, c == NC - 1))
+        def _():
+            x_left(c).wait_send()
+
         for h in range(HALVES):
             here = slice(h * HB, (h + 1) * HB)
             term = dot_nn(w_row[here, :BLK], q0[c]) + dot_nn(w_row[here, BLK:2 * BLK], xr_in[c])
             send_l[c, here, :] = term.astype(BF16)
         t_left(c).start()
-        x_right(c).wait_send()
+        @pl.when(jnp.logical_or(order["r"] == 1, c == NC - 1))
+        def _():
+            x_right(c).wait_send()
+
         for h in range(HALVES):
             here = slice(h * HB, (h + 1) * HB)
             term = dot_nn(w_row[here, 2 * BLK:3 * BLK], q0[c]) + dot_nn(w_row[here, 3 * BLK:], xl_in[c])
@@ -379,7 +423,8 @@
             pltpu.VMEM((2, BLK, CW), BF16),
         ]
         + [dma((NC,))] * 14
-        + [dma((2,))] * 3,
+        + [dma((2,))] * 3
+        + [pltpu.SemaphoreType.REGULAR((2,))],
         compiler_params=pltpu.CompilerParams(
             collective_id=0, has_side_effects=True, vmem_limit_bytes=VM * 1024 * 1024
         ),

time: 315 us -> 295 us (0.937)
  Pallas kernels: 306 us -> 284 us
    pallas_call x1, Pallas kernels: 306 us -> 284 us  [per_device(): pl.pallas_call(exchange_kernel, out_shape=(jax.ShapeDtypeStruct((BLK, D),...]
where the time goes in v2:
time: 295 us; the launch traced here: 292 us
  Pallas kernels  284 us (96%)
  local copies, waits for them, and re-layouts  7.45 us (3%)
    pallas_call x1, Pallas kernels, per_device(): pl.pallas_call(exchange_kernel, out_shape=(jax.ShapeDtypeStruct((BLK, D),...  284 us
    unnamed x7, local copies, waits for them, and re-layouts  7.45 us

profile of v2, /device:TPU:24, one launch (start us, length us, event | category | flops | bytes accessed | tf_op | source)
XLA Modules:
  0.0 292.4 jit_solution(11600229741562952430)
XLA Ops:
  0.6 284.3 %shard_map.67 = (bf16[512,4096]{1,0:T(8,128)(2,1)}, bf16[512,4096]{1,0:T(8,128)(2,1)}, f32[1,512]{1,0:T(1,128)}) custom-call(s32[64]{0:T(128)} %sizes_ref.1, s32[1,512]{1,0:T(1,128)} %pos_ref.1, bf16[512,4096]{1,0:T(8,128)(2,1)} %q_hbm.1, bf16[512,4096]{1,0:T(8,128)(2,1)} %p_hbm.1), custom_call_target="tpu_custom_call" | custom-call | flops 49999998976 | bytes 67108864 | tf_op jit(solution)/shard_map/pallas_call | solution.py:404
  284.9 0.0 copy-start
  285.0 4.8 %copy.10 = bf16[512,4096]{1,0:T(8,128)(2,1)} copy(bf16[512,4096]{1,0:T(8,128)(2,1)} %get-tuple-element.6) | data formatting | bytes 8388608
  289.8 0.0 copy-done
  289.8 0.0 copy-start.1
  289.8 2.0 copy.11
  291.8 0.0 copy-done.1
  291.8 0.6 copy.12
Async XLA Ops:
  284.9 4.9 %copy-start = (bf16[512,4096]{1,0:T(8,128)(2,1)S(1)}, bf16[512,4096]{1,0:T(8,128)(2,1)}, u32[]{:S(2)}) copy-start(bf16[512,4096]{1,0:T(8,128)(2,1)} %get-tuple-element.7) | copy-start | bytes 12582916
  289.8 2.0 copy-start.1

commit v3 on v2

--- a/solution.py
+++ b/solution.py
@@ -39,7 +39,7 @@
     sizes_ref, pos_ref, q_hbm, p_hbm,
     gq_hbm, gp_hbm, loss_ref,
     q0, p0, pl_in, pr_in, xl_in, xr_in, tl_in, tr_in, send_r, send_l,
-    s3, row_lse, col_lse, msg_l, msg_r, pos_t, w_row, wt_p, stage,
+    s3, row_lse, col_peak, col_sum, col_lse, msg_l, msg_r, pos_t, w_row, wt_p, stage,
     sem_q, sem_p, ps_r, ps_l, pr_r, pr_l, xs_r, xs_l, xr_r, xr_l, ts_r, ts_l, tr_r, tr_l,
     msg_send, msg_recv, out_sem, token,
 ):
@@ -125,8 +125,9 @@
     far_r = jnp.where(me < NB - 2, 1 - at_after, 0) * has_r
     rows_l = has_l - far_l
     rows_r = has_r - far_r
-
-    def add_scores(r, k, c, a_ref, b_ref):
+    end = far_l + far_r
+
+    def add_scores(r, k, c, a_ref, b_ref, held):
         for h in range(HALVES):
             ref = s3.at[pl.ds(r * BLK + h * HB, HB), pl.ds(k * BLK, BLK)]
             part = dot_nt(a_ref[c, h * HB:(h + 1) * HB, :], b_ref[c])
@@ -135,15 +136,57 @@
             def _():
                 ref[...] = part
 
-            @pl.when(c > 0)
+            @pl.when(jnp.logical_and(c > 0, c < NC - 1))
             def _():
                 ref[...] += part
 
+            @pl.when(c == NC - 1)
+            def _():
+                ref[...] = jnp.where(mask_of(held, (HB, BLK)), (ref[...] + part) * SCALE, LOWEST)
+
+    held_rows = (rows_l, jnp.int32(1), rows_r)
+    held_cols = (has_l, jnp.int32(1), has_r)
+    RT = 64
+
+    def block_row_stats(r):
+        def step(t, carry):
+            rows = pl.ds(pl.multiple_of(r * BLK + t * RT, RT), RT)
+            top = jnp.full((RT, 128), LOWEST, F32)
+            for k in range(12):
+                top = jnp.maximum(top, s3[rows, k * 128:(k + 1) * 128])
+            top = jnp.max(top, axis=1, keepdims=True)
+            total = jnp.zeros((RT, 128), F32)
+            out = []
+            for k in range(3):
+                tile = s3[rows, k * BLK:(k + 1) * BLK]
+                part = jnp.exp(tile - top)
+                for j in range(4):
+                    total = total + part[:, j * 128:(j + 1) * 128]
+                old_peak, old_sum = carry[2 * k], carry[2 * k + 1]
+                split = tile.reshape(RT // 8, 8, BLK)
+                peak = jnp.maximum(old_peak, jnp.max(split, axis=0))
+                out.append(peak)
+                out.append(old_sum * jnp.exp(old_peak - peak) + jnp.sum(jnp.exp(split - peak[None]), axis=0))
+            lse = top + jnp.log(jnp.sum(total, axis=1, keepdims=True))
+            row_lse[rows, :] = jnp.broadcast_to(lse, (RT, 128))
+            return tuple(out)
+
+        carry = []
+        for k in range(3):
+            carry += [col_peak[:, k * BLK:(k + 1) * BLK], col_sum[:, k * BLK:(k + 1) * BLK]]
+        carry = lax.fori_loop(0, BLK // RT, step, tuple(carry))
+        for k in range(3):
+            col_peak[:, k * BLK:(k + 1) * BLK] = carry[2 * k]
+            col_sum[:, k * BLK:(k + 1) * BLK] = carry[2 * k + 1]
+
+    col_peak[...] = jnp.full((8, 3 * BLK), LOWEST, F32)
+    col_sum[...] = jnp.zeros((8, 3 * BLK), F32)
+
     @pl.loop(0, NC)
     def _(c):
         q_load(c).wait()
         p_load(c).wait()
-        add_scores(1, 1, c, q0, p0)
+        add_scores(1, 1, c, q0, p0, jnp.int32(1))
 
     @pl.loop(0, NC)
     def _(c):
@@ -163,10 +206,11 @@
         def _():
             x_left(c).start()
 
-        add_scores(1, 0, c, q0, pl_in)
-        add_scores(1, 2, c, q0, pr_in)
+        add_scores(1, 0, c, q0, pl_in, has_l)
+        add_scores(1, 2, c, q0, pr_in, has_r)
 
     send_x = {"r": x_right, "l": x_left}
+    block_row_stats(1)
 
     @pl.loop(0, NC)
     def _(c):
@@ -192,50 +236,15 @@
         x_left(c).wait_recv()
         for r, x_in in ((0, xl_in), (2, xr_in)):
             for k, p_in in ((0, pl_in), (1, p0), (2, pr_in)):
-                add_scores(r, k, c, x_in, p_in)
-
-    held_rows = (rows_l, jnp.int32(1), rows_r)
-    held_cols = (has_l, jnp.int32(1), has_r)
-    RT = 64
-
-    def valid(r, k, shape):
-        return mask_of(held_rows[r] * held_cols[k], shape)
-
-    col_peak = [jnp.full((8, BLK), LOWEST, F32) for _ in range(3)]
-    for r in range(3):
-        def peaks(t, peak):
-            rows = pl.ds(pl.multiple_of(r * BLK + t * RT, RT), RT)
-            tiles = [
-                jnp.where(valid(r, k, (RT, BLK)), s3[rows, k * BLK:(k + 1) * BLK] * SCALE, LOWEST)
-                for k in range(3)
-            ]
-            top = jnp.max(jnp.maximum(jnp.maximum(tiles[0], tiles[1]), tiles[2]), axis=1, keepdims=True)
-            total = jnp.zeros((RT, 1), F32)
-            for tile in tiles:
-                total = total + jnp.sum(jnp.exp(tile - top), axis=1, keepdims=True)
-            row_lse[rows, :] = jnp.broadcast_to(top + jnp.log(total), (RT, 128))
-            return tuple(
-                jnp.maximum(old, jnp.max(tile.reshape(RT // 8, 8, BLK), axis=0))
-                for old, tile in zip(peak, tiles)
-            )
-
-        col_peak = lax.fori_loop(0, BLK // RT, peaks, tuple(col_peak))
-    col_top = [jnp.max(peak, axis=0, keepdims=True) for peak in col_peak]
-    col_sum = [jnp.zeros((8, BLK), F32) for _ in range(3)]
-    for r in range(3):
-        def sums(t, total):
-            rows = pl.ds(pl.multiple_of(r * BLK + t * RT, RT), RT)
-            out = []
-            for k in range(3):
-                tile = jnp.where(valid(r, k, (RT, BLK)), s3[rows, k * BLK:(k + 1) * BLK] * SCALE, LOWEST)
-                part = jnp.exp(tile - col_top[k])
-                out.append(total[k] + jnp.sum(part.reshape(RT // 8, 8, BLK), axis=0))
-            return tuple(out)
-
-        col_sum = lax.fori_loop(0, BLK // RT, sums, tuple(col_sum))
+                add_scores(r, k, c, x_in, p_in, held_rows[r] * held_cols[k])
+
+    block_row_stats(0)
+    block_row_stats(2)
     for k in range(3):
-        lse = col_top[k] + jnp.log(jnp.sum(col_sum[k], axis=0, keepdims=True))
-        col_lse[:, k * BLK:(k + 1) * BLK] = jnp.broadcast_to(lse, (8, BLK))
+        here = slice(k * BLK, (k + 1) * BLK)
+        peak = jnp.max(col_peak[:, here], axis=0, keepdims=True)
+        total = jnp.sum(col_sum[:, here] * jnp.exp(col_peak[:, here] - peak), axis=0, keepdims=True)
+        col_lse[:, here] = jnp.broadcast_to(peak + jnp.log(total), (8, BLK))
 
     tell_r = remote(col_lse, msg_l, msg_send.at[0], msg_recv.at[0], right)
     tell_l = remote(col_lse, msg_r, msg_send.at[1], msg_recv.at[1], left)
@@ -252,7 +261,7 @@
         @pl.loop(0, 4)
         def _(t):
             rows = pl.ds(pl.multiple_of(r * BLK + t * 128, 128), 128)
-            tile = s3[rows, k * BLK:(k + 1) * BLK] * SCALE
+            tile = s3[rows, k * BLK:(k + 1) * BLK]
             value = weight_tile(tile, row_lse[rows, 0:1], lse_cols)
             value = jnp.where(mask_of(ok, value.shape), value, 0.0)
             out[:, pl.ds(pl.multiple_of(at + t * 128, 128), 128)] = value.T.astype(BF16)
@@ -286,11 +295,10 @@
         for h in range(HALVES):
             here = slice(h * HB, (h + 1) * HB)
             xl_in[c, here, :] = jnp.where(mask_of(far_r, (HB, CW)), xr_in[c, here, :], xl_in[c, here, :])
-        add_scores(0, 0, c, q0, xl_in)
+        add_scores(0, 0, c, q0, xl_in, end)
 
     tell_r.wait()
     tell_l.wait()
-    end = far_l + far_r
 
     def pick(from_left, from_right, own):
         out = own
@@ -314,8 +322,7 @@
         here = pl.ds(pl.multiple_of(t * WT, WT), WT)
         own = pl.ds(pl.multiple_of(BLK + t * WT, WT), WT)
         shape = (WT, BLK)
-        raw = [s3[own, k * BLK:(k + 1) * BLK] * SCALE for k in range(3)] + [s3[here, :BLK] * SCALE]
-        tiles = [jnp.where(mask_of(flag, shape), tile, LOWEST) for flag, tile in zip(flags, raw)]
+        tiles = [s3[own, k * BLK:(k + 1) * BLK] for k in range(3)] + [s3[here, :BLK]]
         top = jnp.max(
             jnp.maximum(jnp.maximum(tiles[0], tiles[1]), jnp.maximum(tiles[2], tiles[3])), axis=1, keepdims=True
         )
@@ -325,10 +332,10 @@
         lse_rows = top + jnp.log(total)
         lane = lax.broadcasted_iota(jnp.int32, shape, 1).astype(F32)
         onehot = jnp.concatenate([pos_t[here, :]] * 4, axis=1) == lane
-        hits = jnp.where(onehot, lse_0 - 2.0 * raw[1], 0.0)
+        hits = jnp.where(onehot, lse_0 - 2.0 * tiles[1], 0.0)
         loss = lse_rows + jnp.sum(hits, axis=1, keepdims=True)
         loss_ref[:, here] = jnp.broadcast_to(loss, (WT, 128)).T[0:1, :]
-        for k, (flag, tile, lse_cols) in enumerate(zip(flags, raw, (lse_l, lse_0, lse_r, lse_x))):
+        for k, (flag, tile, lse_cols) in enumerate(zip(flags, tiles, (lse_l, lse_0, lse_r, lse_x))):
             value = weight_tile(tile, lse_rows, lse_cols)
             if k == 1:
                 value = jnp.where(onehot, value - 2.0, value)
@@ -417,6 +424,8 @@
             pltpu.VMEM((8, 3 * BLK), F32),
             pltpu.VMEM((8, 3 * BLK), F32),
             pltpu.VMEM((8, 3 * BLK), F32),
+            pltpu.VMEM((8, 3 * BLK), F32),
+            pltpu.VMEM((8, 3 * BLK), F32),
             pltpu.VMEM((BLK, 128), F32),
             pltpu.VMEM((BLK, 4 * BLK), BF16),
             pltpu.VMEM((BLK, 3 * BLK), BF16),

time: 295 us -> 295 us (level)
  no operation moved by 1% of the time
where the time goes in v3:
time: 295 us; the launch traced here: 291 us
  Pallas kernels  283 us (96%)
  local copies, waits for them, and re-layouts  7.45 us (3%)
    pallas_call x1, Pallas kernels, per_device(): pl.pallas_call(exchange_kernel, out_shape=(jax.ShapeDtypeStruct((BLK, D),...  283 us
    unnamed x7, local copies, waits for them, and re-layouts  7.45 us

profile of v3, /device:TPU:24, one launch (start us, length us, event | category | flops | bytes accessed | tf_op | source)
XLA Modules:
  0.0 291.2 jit_solution(8198601311636907313)
XLA Ops:
  0.6 283.1 %shard_map.67 = (bf16[512,4096]{1,0:T(8,128)(2,1)}, bf16[512,4096]{1,0:T(8,128)(2,1)}, f32[1,512]{1,0:T(1,128)}) custom-call(s32[64]{0:T(128)} %sizes_ref.1, s32[1,512]{1,0:T(1,128)} %pos_ref.1, bf16[512,4096]{1,0:T(8,128)(2,1)} %q_hbm.1, bf16[512,4096]{1,0:T(8,128)(2,1)} %p_hbm.1), custom_call_target="tpu_custom_call" | custom-call | flops 49999998976 | bytes 67108864 | tf_op jit(solution)/shard_map/pallas_call | solution.py:411
  283.8 0.0 copy-start
  283.8 4.8 %copy.10 = bf16[512,4096]{1,0:T(8,128)(2,1)} copy(bf16[512,4096]{1,0:T(8,128)(2,1)} %get-tuple-element.6) | data formatting | bytes 8388608
  288.6 0.0 copy-done
  288.6 0.0 copy-start.1
  288.6 2.0 copy.11
  290.7 0.0 copy-done.1
  290.7 0.6 copy.12
Async XLA Ops:
  283.8 4.9 %copy-start = (bf16[512,4096]{1,0:T(8,128)(2,1)S(1)}, bf16[512,4096]{1,0:T(8,128)(2,1)}, u32[]{:S(2)}) copy-start(bf16[512,4096]{1,0:T(8,128)(2,1)} %get-tuple-element.7) | copy-start | bytes 12582916
  288.6 2.0 copy-start.1

commit v4 on v2

--- a/solution.py
+++ b/solution.py
@@ -373,13 +373,16 @@
         def _():
             gp_out(c - 2, slot).wait()
 
+        shape = (HB, CW)
+        totals = []
+        for h in range(HALVES):
+            here = slice(h * HB, (h + 1) * HB)
+            total = dot_nn(wt_p[here, :BLK], q0[c]) + dot_nn(wt_p[here, BLK:2 * BLK], xl_in[c])
+            totals.append(total + dot_nn(wt_p[here, 2 * BLK:], xr_in[c]))
         t_right(c).wait_recv()
         t_left(c).wait_recv()
-        shape = (HB, CW)
-        for h in range(HALVES):
-            here = slice(h * HB, (h + 1) * HB)
-            total = dot_nn(wt_p[here, :BLK], q0[c]) + dot_nn(wt_p[here, BLK:2 * BLK], xl_in[c])
-            total = total + dot_nn(wt_p[here, 2 * BLK:], xr_in[c])
+        for h, total in enumerate(totals):
+            here = slice(h * HB, (h + 1) * HB)
             total = total + jnp.where(mask_of(far_l, shape), tl_in[c, here, :].astype(F32), 0.0)
             total = total + jnp.where(mask_of(far_r, shape), tr_in[c, here, :].astype(F32), 0.0)
             stage[slot, here, :] = total.astype(BF16)

time: 295 us -> 294 us (level)
  no operation moved by 1% of the time
where the time goes in v4:
time: 294 us; the launch traced here: 292 us
  Pallas kernels  284 us (97%)
  local copies, waits for them, and re-layouts  7.45 us (3%)
    pallas_call x1, Pallas kernels, per_device(): pl.pallas_call(exchange_kernel, out_shape=(jax.ShapeDtypeStruct((BLK, D),...  284 us
    unnamed x7, local copies, waits for them, and re-layouts  7.45 us

profile of v4, /device:TPU:24, one launch (start us, length us, event | category | flops | bytes accessed | tf_op | source)
XLA Modules:
  0.0 291.6 jit_solution(1762493341412893071)
XLA Ops:
  0.6 283.5 %shard_map.67 = (bf16[512,4096]{1,0:T(8,128)(2,1)}, bf16[512,4096]{1,0:T(8,128)(2,1)}, f32[1,512]{1,0:T(1,128)}) custom-call(s32[64]{0:T(128)} %sizes_ref.1, s32[1,512]{1,0:T(1,128)} %pos_ref.1, bf16[512,4096]{1,0:T(8,128)(2,1)} %q_hbm.1, bf16[512,4096]{1,0:T(8,128)(2,1)} %p_hbm.1), custom_call_target="tpu_custom_call" | custom-call | flops 49999998976 | bytes 67108864 | tf_op jit(solution)/shard_map/pallas_call | solution.py:407
  284.1 0.0 copy-start
  284.2 4.8 %copy.10 = bf16[512,4096]{1,0:T(8,128)(2,1)} copy(bf16[512,4096]{1,0:T(8,128)(2,1)} %get-tuple-element.6) | data formatting | bytes 8388608
  289.0 0.0 copy-done
  289.0 0.0 copy-start.1
  289.0 2.0 copy.11
  291.0 0.0 copy-done.1
  291.0 0.6 copy.12
Async XLA Ops:
  284.1 4.9 %copy-start = (bf16[512,4096]{1,0:T(8,128)(2,1)S(1)}, bf16[512,4096]{1,0:T(8,128)(2,1)}, u32[]{:S(2)}) copy-start(bf16[512,4096]{1,0:T(8,128)(2,1)} %get-tuple-element.7) | copy-start | bytes 12582916
  289.0 2.0 copy-start.1

commit v5 on v4

--- a/solution.py
+++ b/solution.py
@@ -56,6 +56,13 @@
     barrier = pltpu.get_barrier_semaphore()
     for neighbour in (left, right, twin):
         pl.semaphore_signal(barrier, inc=1, device_id=neighbour, device_id_type=MESH)
+
+    @pl.loop(0, NC)
+    def _(c):
+        here = pl.ds(pl.multiple_of(c * CW, CW), CW)
+        pltpu.make_async_copy(q_hbm.at[:, here], q0.at[c], sem_q.at[c]).start()
+        pltpu.make_async_copy(p_hbm.at[:, here], p0.at[c], sem_p.at[c]).start()
+
     pl.semaphore_wait(barrier, 3)
 
     WAYS = ("r", "l")
@@ -102,8 +109,6 @@
     def _(c):
         p_right(c).start()
         p_left(c).start()
-        q_load(c).start()
-        p_load(c).start()
 
     def scan_sizes(k, carry):
         end, at_me, at_next, at_before, at_after = carry

time: 294 us -> 294 us (level)
  no operation moved by 1% of the time
where the time goes in v5:
time: 294 us; the launch traced here: 292 us
  Pallas kernels  284 us (97%)
  local copies, waits for them, and re-layouts  7.45 us (3%)
    pallas_call x1, Pallas kernels, per_device(): pl.pallas_call(exchange_kernel, out_shape=(jax.ShapeDtypeStruct((BLK, D),...  284 us
    unnamed x7, local copies, waits for them, and re-layouts  7.45 us

profile of v5, /device:TPU:24, one launch (start us, length us, event | category | flops | bytes accessed | tf_op | source)
XLA Modules:
  0.0 291.6 jit_solution(16970154999476519946)
XLA Ops:
  0.6 283.5 %shard_map.67 = (bf16[512,4096]{1,0:T(8,128)(2,1)}, bf16[512,4096]{1,0:T(8,128)(2,1)}, f32[1,512]{1,0:T(1,128)}) custom-call(s32[64]{0:T(128)} %sizes_ref.1, s32[1,512]{1,0:T(1,128)} %pos_ref.1, bf16[512,4096]{1,0:T(8,128)(2,1)} %q_hbm.1, bf16[512,4096]{1,0:T(8,128)(2,1)} %p_hbm.1), custom_call_target="tpu_custom_call" | custom-call | flops 49999998976 | bytes 67108864 | tf_op jit(solution)/shard_map/pallas_call | solution.py:412
  284.1 0.0 copy-start
  284.2 4.8 %copy.10 = bf16[512,4096]{1,0:T(8,128)(2,1)} copy(bf16[512,4096]{1,0:T(8,128)(2,1)} %get-tuple-element.6) | data formatting | bytes 8388608
  289.0 0.0 copy-done
  289.0 0.0 copy-start.1
  289.0 2.0 copy.11
  291.0 0.0 copy-done.1
  291.0 0.6 copy.12
Async XLA Ops:
  284.1 4.9 %copy-start = (bf16[512,4096]{1,0:T(8,128)(2,1)S(1)}, bf16[512,4096]{1,0:T(8,128)(2,1)}, u32[]{:S(2)}) copy-start(bf16[512,4096]{1,0:T(8,128)(2,1)} %get-tuple-element.7) | copy-start | bytes 12582916
  289.0 2.0 copy-start.1
